TPU v7x, 32 devices: a whole 2x2x4 slice. The times are simulated.
32 devices in a mesh: chan: 8 (over z, y), tm: 4 (over x, core).
Axes of the slice: x: 2, y: 2, z: 4, core: 2. Of those that a mesh axis runs over, the one named last changes fastest.
Arguments:
- record: float32 [64, 256, 16384], P('tm', 'chan'), may hold values from -6 to 6
- fir_taps: float32 [64], replicated, may hold values from -0.75 to 0.75
- pair_offsets: int32 [8], replicated, may hold values from -128 to 128, as said below
Outputs:
- correlation: float32 [8, 256, 16384], P('tm', None, 'chan')
Inputs may be any that keep to these rules, and one draw needn't show every extreme that they name: `pair_offsets`: 8 distinct nonzero channel offsets; both -128 and 128 are among them.
All inputs are finite; a program needn't handle non-finite values.
Results may differ from a plain program's by a relative error of at most 0.000098.
Values sent between devices are 32-bit elements; how exact they have to be, the bound alone decides.
A program may use at most 320 MiB of HBM per device.

v0:
```python
import math

import jax
import jax.numpy as jnp
from jax import lax
from jax.sharding import PartitionSpec as P

S = 256
R = 128


PRECISE = lax.Precision.HIGHEST


def extended(array, sides, width):
    for axis, dim in sides:
        size, length = (lax.axis_size(axis), array.shape[dim])
        up = [(i, (i + 1) % size) for i in range(size)]
        down = [(j, i) for i, j in up]
        last = lax.slice_in_dim(array, length - width, length, axis=dim)
        first = lax.slice_in_dim(array, 0, width, axis=dim)
        before = lax.ppermute(last, axis, up)
        after = lax.ppermute(first, axis, down)
        array = jnp.concatenate([before, array, after], axis=dim)
    return array


def fir_matrix_of(fir_taps, seg_len):
    row_ids = lax.broadcasted_iota(jnp.int32, (seg_len, seg_len), 0)
    col_ids = lax.broadcasted_iota(jnp.int32, (seg_len, seg_len), 1)
    spread = col_ids - row_ids

    def add_tap(tap_number, running):
        return running + jnp.where(spread == tap_number, fir_taps[tap_number], 0.0)

    return lax.fori_loop(0, fir_taps.shape[0], add_tap, jnp.zeros((seg_len, seg_len), jnp.float32))


def forward_table(seg_len):
    length = 2 * seg_len
    time_ids = lax.broadcasted_iota(jnp.int32, (seg_len, length), 0)
    slot_ids = lax.broadcasted_iota(jnp.int32, (seg_len, length), 1)
    frequency = jnp.where(slot_ids <= seg_len, slot_ids, slot_ids - seg_len)
    angles = (frequency * time_ids % length).astype(jnp.float32) * (2.0 * math.pi / length)
    return jnp.where(slot_ids <= seg_len, jnp.cos(angles), jnp.sin(angles))


def inverse_table(seg_len, norm_scale):
    length = 2 * seg_len
    slot_ids = lax.broadcasted_iota(jnp.int32, (3 * seg_len, seg_len), 0)
    lag_ids = lax.broadcasted_iota(jnp.int32, (3 * seg_len, seg_len), 1) - seg_len // 2
    cosine_rows = slot_ids < length
    frequency = jnp.where(
        cosine_rows, jnp.where(slot_ids <= seg_len, slot_ids, slot_ids - seg_len), slot_ids - length
    )
    angles = (frequency * lag_ids % length).astype(jnp.float32) * (2.0 * math.pi / length)
    edge_rows = (slot_ids == 0) | (slot_ids == seg_len)
    cosine_weights = jnp.where(edge_rows, 1.0 / length, 2.0 / length)
    sine_weights = jnp.where(frequency == 0, 0.0, -2.0 / length)
    values = jnp.where(
        cosine_rows, cosine_weights * jnp.cos(angles), sine_weights * jnp.sin(angles)
    )
    return values * norm_scale


def per_device(record, fir_taps, pair_offsets):
    n_chan = lax.axis_size("chan")
    n_time = lax.axis_size("tm")
    seg_count, part_rows, channels = record.shape
    block_width = channels // n_chan
    fir_matrix = fir_matrix_of(fir_taps, S)
    forward = forward_table(S)
    turned = lax.all_to_all(record, "chan", split_axis=2, concat_axis=1, tiled=True)
    widened = extended(turned, (("chan", 2),), R)
    whitened = jnp.einsum("ut,suc->stc", fir_matrix, widened, precision=PRECISE)
    spectra = jnp.einsum("stc,tj->scj", whitened, forward, precision=PRECISE)
    own_spec = spectra[:, R : R + block_width, :]
    norm_scale = 1.0 / math.sqrt(seg_count * n_time * S)
    inverse = inverse_table(S, norm_scale)
    inverse_cos = inverse[: 2 * S]
    inverse_sin = inverse[2 * S :]

    def one_offset(offset):
        partner = lax.dynamic_slice_in_dim(spectra, R + offset, block_width, axis=1)
        matched = jnp.sum(own_spec * partner, axis=0)
        skew_part = jnp.sum(
            own_spec[:, :, S:] * partner[:, :, :S] - own_spec[:, :, :S] * partner[:, :, S:], axis=0
        )
        cos_terms = jnp.einsum("rl,cr->lc", inverse_cos, matched, precision=PRECISE)
        sin_terms = jnp.einsum("rl,cr->lc", inverse_sin, skew_part, precision=PRECISE)
        return cos_terms + sin_terms

    return lax.psum_scatter(
        lax.map(one_offset, pair_offsets), "tm", scatter_dimension=0, tiled=True
    )


def solution(mesh):
    placed = (P("tm", "chan", None), P(), P())
    return jax.shard_map(
        per_device, mesh=mesh, in_specs=placed, out_specs=P("tm", None, "chan"), check_vma=False
    )
```

profile of v0, /device:TPU:15, one launch (start us, length us, event | category | flops | bytes accessed | tf_op | source)
XLA Modules:
  0.0 2460.7 jit_solution(4328524203799009892)
XLA Ops:
  6.5 86.1 %copy.11 = f32[16,32,16384]{1,0,2:T(8,128)} copy(f32[16,32,16384]{2,1,0:T(8,128)} %param.7) | data formatting | bytes 67108864 | tf_op args[0]
  92.6 120.3 %reshape.6 = f32[8,1,1048576]{2,1,0:T(1,128)} reshape(f32[16384,16,32]{2,1,0:T(8,128)} %bitcast.21) | data formatting | bytes 67108864
  220.0 719.8 %all-to-all-done = f32[8,1,1048576]{2,1,0:T(1,128)} async-done(((f32[8,1,1048576]{2,1,0:T(1,128)}), f32[8,1,1048576]{2,1,0:T(1,128)}, u32[]{:S(2)}, u32[]{:S(2)}) %all-to-all-start) | async-done | bytes 33554464 | tf_op jit(solution)/shard_map/all_to_all | solution.py:73
  940.3 98.3 %reduce = f32[8,1048576]{1,0:T(8,128)} reduce(f32[8,1,1048576]{2,1,0:T(1,128)} %all-to-all-done, f32[]{:T(128)} %broadcast.92), dimensions={1}, to_apply=%all_to_all.13.reduce_sub_computation | reduce | bytes 67108864 | tf_op jit(solution)/shard_map/all_to_all | solution.py:73
  1038.6 165.5 %reshape.7 = f32[16384,16,32]{2,1,0:T(8,128)} reshape(f32[8,1048576]{1,0:T(8,128)} %reduce) | data formatting | bytes 67108864
  1204.1 83.7 %copy.13 = f32[16,8,32,2048]{3,2,1,0:T(8,128)} copy(f32[16,8,32,2048]{2,0,3,1:T(8,128)} %bitcast.6) | data formatting | bytes 67108864 | tf_op jit(solution)/shard_map/all_to_all | solution.py:73
  1325.8 86.5 %while.27 = (s32[]{:T(128)}, f32[256,256]{1,0:T(8,128)S(1)}, f32[64]{0:T(128)S(1)}, s32[]{:T(128)}, s32[]{:T(128)}) while((s32[]{:T(128)}, f32[256,256]{1,0:T(8,128)S(1)}, f32[64]{0:T(128)S(1)}, s32[]{:T(128)}, s32[]{:T(128)}) %tuple.65), condition=%wide.region_1.2_spmd.clone, body=%wide.region_0.1_spmd.clone.sunk | while | flops 327683 | bytes 524379 | solution.py:36
  1453.5 68.4 %fusion.11 = f32[16,2304,512]{2,1,0:T(8,128)} fusion(f32[16,2304,256]{2,1,0:T(8,128)} %fusion.5, f32[256,512,1]{1,0,2:T(8,128)S(1)} %fusion.54), kind=kOutput, calls=%fused_computation.17 | convolution fusion | flops 57982058496 | bytes 113770496 | tf_op jit(solution)/shard_map/stc,tj->scj/dot_general | solution.py:76
  1521.9 43.3 %slice.46 = f32[16,2048,512]{2,1,0:T(8,128)} slice(f32[16,2304,512]{2,1,0:T(8,128)} %fusion.11), slice={[0:16], [128:2176], [0:512]} | slice | bytes 134217728 | tf_op jit(solution)/shard_map/slice | solution.py:77
  1565.2 759.6 %while.26 = (s32[]{:T(128)}, f32[8,256,2048]{2,1,0:T(8,128)}, s32[8]{0:T(128)S(1)}, f32[16,2304,512]{2,1,0:T(8,128)}, f32[16,2048,512]{2,1,0:T(8,128)}, /*index=...) while((s32[]{:T(128)}, f32[8,256,2048]{2,1,0:T(8,128)}, ...), condition=%wide.region_5.6_spmd, body=%wide.region_2.5_spmd.sunk | while | flops 4897898496 | bytes 296485536 | solution.py:94
  1567.4 41.3 %multiply_reduce_fusion.2 = f32[2048,512]{1,0:T(8,128)S(1)} fusion(f32[16,2048,512]{2,1,0:T(8,128)} %get-tuple-element.320, f32[16,2304,512]{2,1,0:T(8,128)} %get-tuple-element.319, s32[]{:T(128)S(6)} %select_n.137), kind=kLoop, calls=%fused_computation.1.clone.1 | loop fusion | flops 32505856 | bytes 138412032 | tf_op jit(solution)/shard_map/while/body/eval_jaxpr/reduce_sum | solution.py:85
  1612.2 41.9 %fusion.68 = f32[2048,256]{1,0:T(8,128)S(1)} fusion(f32[16,2304,512]{2,1,0:T(8,128)} %get-tuple-element.319, s32[]{:T(128)S(6)} %select_n.137, s32[]{:T(128)S(6)} %add.125, f32[16,2048,512]{2,1,0:T(8,128)} %get-tuple-element.320), kind=kLoop, calls=%fused_computation.4.clone.1 | loop fusion | flops 33030144 | bytes 136314880 | tf_op jit(solution)/shard_map/while/body/eval_jaxpr/reduce_sum | solution.py:86
  1662.5 41.3 %multiply_reduce_fusion.2 = f32[2048,512]{1,0:T(8,128)S(1)} fusion(f32[16,2048,512]{2,1,0:T(8,128)} %get-tuple-element.320, f32[16,2304,512]{2,1,0:T(8,128)} %get-tuple-element.319, s32[]{:T(128)S(6)} %select_n.137), kind=kLoop, calls=%fused_computation.1.clone.1 | loop fusion | flops 32505856 | bytes 138412032 | tf_op jit(solution)/shard_map/while/body/eval_jaxpr/reduce_sum | solution.py:85
  1707.3 41.8 %fusion.68 = f32[2048,256]{1,0:T(8,128)S(1)} fusion(f32[16,2304,512]{2,1,0:T(8,128)} %get-tuple-element.319, s32[]{:T(128)S(6)} %select_n.137, s32[]{:T(128)S(6)} %add.125, f32[16,2048,512]{2,1,0:T(8,128)} %get-tuple-element.320), kind=kLoop, calls=%fused_computation.4.clone.1 | loop fusion | flops 33030144 | bytes 136314880 | tf_op jit(solution)/shard_map/while/body/eval_jaxpr/reduce_sum | solution.py:86
  1802.2 41.7 %fusion.68 = f32[2048,256]{1,0:T(8,128)S(1)} fusion(f32[16,2304,512]{2,1,0:T(8,128)} %get-tuple-element.319, s32[]{:T(128)S(6)} %select_n.137, s32[]{:T(128)S(6)} %add.125, f32[16,2048,512]{2,1,0:T(8,128)} %get-tuple-element.320), kind=kLoop, calls=%fused_computation.4.clone.1 | loop fusion | flops 33030144 | bytes 136314880 | tf_op jit(solution)/shard_map/while/body/eval_jaxpr/reduce_sum | solution.py:86
  1852.3 41.3 %multiply_reduce_fusion.2 = f32[2048,512]{1,0:T(8,128)S(1)} fusion(f32[16,2048,512]{2,1,0:T(8,128)} %get-tuple-element.320, f32[16,2304,512]{2,1,0:T(8,128)} %get-tuple-element.319, s32[]{:T(128)S(6)} %select_n.137), kind=kLoop, calls=%fused_computation.1.clone.1 | loop fusion | flops 32505856 | bytes 138412032 | tf_op jit(solution)/shard_map/while/body/eval_jaxpr/reduce_sum | solution.py:85
  1897.0 41.8 %fusion.68 = f32[2048,256]{1,0:T(8,128)S(1)} fusion(f32[16,2304,512]{2,1,0:T(8,128)} %get-tuple-element.319, s32[]{:T(128)S(6)} %select_n.137, s32[]{:T(128)S(6)} %add.125, f32[16,2048,512]{2,1,0:T(8,128)} %get-tuple-element.320), kind=kLoop, calls=%fused_computation.4.clone.1 | loop fusion | flops 33030144 | bytes 136314880 | tf_op jit(solution)/shard_map/while/body/eval_jaxpr/reduce_sum | solution.py:86
  1991.8 41.6 %fusion.68 = f32[2048,256]{1,0:T(8,128)S(1)} fusion(f32[16,2304,512]{2,1,0:T(8,128)} %get-tuple-element.319, s32[]{:T(128)S(6)} %select_n.137, s32[]{:T(128)S(6)} %add.125, f32[16,2048,512]{2,1,0:T(8,128)} %get-tuple-element.320), kind=kLoop, calls=%fused_computation.4.clone.1 | loop fusion | flops 33030144 | bytes 136314880 | tf_op jit(solution)/shard_map/while/body/eval_jaxpr/reduce_sum | solution.py:86
  2041.8 41.2 %multiply_reduce_fusion.2 = f32[2048,512]{1,0:T(8,128)S(1)} fusion(f32[16,2048,512]{2,1,0:T(8,128)} %get-tuple-element.320, f32[16,2304,512]{2,1,0:T(8,128)} %get-tuple-element.319, s32[]{:T(128)S(6)} %select_n.137), kind=kLoop, calls=%fused_computation.1.clone.1 | loop fusion | flops 32505856 | bytes 138412032 | tf_op jit(solution)/shard_map/while/body/eval_jaxpr/reduce_sum | solution.py:85
  2086.6 41.8 %fusion.68 = f32[2048,256]{1,0:T(8,128)S(1)} fusion(f32[16,2304,512]{2,1,0:T(8,128)} %get-tuple-element.319, s32[]{:T(128)S(6)} %select_n.137, s32[]{:T(128)S(6)} %add.125, f32[16,2048,512]{2,1,0:T(8,128)} %get-tuple-element.320), kind=kLoop, calls=%fused_computation.4.clone.1 | loop fusion | flops 33030144 | bytes 136314880 | tf_op jit(solution)/shard_map/while/body/eval_jaxpr/reduce_sum | solution.py:86
  2181.4 41.7 %fusion.68 = f32[2048,256]{1,0:T(8,128)S(1)} fusion(f32[16,2304,512]{2,1,0:T(8,128)} %get-tuple-element.319, s32[]{:T(128)S(6)} %select_n.137, s32[]{:T(128)S(6)} %add.125, f32[16,2048,512]{2,1,0:T(8,128)} %get-tuple-element.320), kind=kLoop, calls=%fused_computation.4.clone.1 | loop fusion | flops 33030144 | bytes 136314880 | tf_op jit(solution)/shard_map/while/body/eval_jaxpr/reduce_sum | solution.py:86
  2231.5 41.4 %multiply_reduce_fusion.2 = f32[2048,512]{1,0:T(8,128)S(1)} fusion(f32[16,2048,512]{2,1,0:T(8,128)} %get-tuple-element.320, f32[16,2304,512]{2,1,0:T(8,128)} %get-tuple-element.319, s32[]{:T(128)S(6)} %select_n.137), kind=kLoop, calls=%fused_computation.1.clone.1 | loop fusion | flops 32505856 | bytes 138412032 | tf_op jit(solution)/shard_map/while/body/eval_jaxpr/reduce_sum | solution.py:85
  2276.3 41.9 %fusion.68 = f32[2048,256]{1,0:T(8,128)S(1)} fusion(f32[16,2304,512]{2,1,0:T(8,128)} %get-tuple-element.319, s32[]{:T(128)S(6)} %select_n.137, s32[]{:T(128)S(6)} %add.125, f32[16,2048,512]{2,1,0:T(8,128)} %get-tuple-element.320), kind=kLoop, calls=%fused_computation.4.clone.1 | loop fusion | flops 33030144 | bytes 136314880 | tf_op jit(solution)/shard_map/while/body/eval_jaxpr/reduce_sum | solution.py:86
  2324.8 128.6 %reduce-scatter.2.cloned.1.call-done = f32[2,256,2048]{2,1,0:T(8,128)} async-done(((f32[8,256,2048]{2,1,0:T(8,128)}), f32[2,256,2048]{2,1,0:T(8,128)}) %reduce-scatter.2.cloned.1.call-update) | async-done | bytes 4194320 | tf_op jit(solution)/shard_map/reduce_scatter | solution.py:93
  (201 shorter events, 380.0 us)
Async XLA Ops:
  212.9 726.9 %all-to-all-start = ((f32[8,1,1048576]{2,1,0:T(1,128)}), f32[8,1,1048576]{2,1,0:T(1,128)}, u32[]{:S(2)}, u32[]{:S(2)}) async-start(f32[8,1,1048576]{2,1,0:T(1,128)} %reshape.6), calls=%async_computation | async-start | bytes 67108864 | tf_op jit(solution)/shard_map/all_to_all | solution.py:73
  220.0 2233.4 %reduce-scatter.2.cloned.1.call-start = ((), (), s32[]{:S(2)}) async-start(), calls=%async_computation.2 | async-start | bytes 20971520 | tf_op jit(solution)/shard_map/reduce_scatter | solution.py:93
  1287.7 38.0 %copy-start.1 = (f32[64]{0:T(128)S(1)}, f32[64]{0:T(128)}, u32[]{:S(2)}) copy-start(f32[64]{0:T(128)} %param.8) | copy-start | bytes 772
  1324.3 93.6 %collective-permute-start = (f32[16,256,128]{1,2,0:T(8,128)}, f32[16,256,128]{1,2,0:T(8,128)}, u32[]{:S(2)}, u32[]{:S(2)}) collective-permute-start(f32[16,256,128]{1,2,0:T(8,128)} %get-tuple-element.209), channel_id=1, source_target_pairs={{0,4},{4,8},{8,12},{12,16},{16,20},{20,24},{24,28},{28,0},{1,5},{5... | collective-permute-start | bytes 6291464 | tf_op jit(solution)/shard_map/ppermute | solution.py:22
  1324.5 93.4 %collective-permute-start.1 = (f32[16,256,128]{1,2,0:T(8,128)}, f32[16,256,128]{1,2,0:T(8,128)}, u32[]{:S(2)}, u32[]{:S(2)}) collective-permute-start(f32[16,256,128]{1,2,0:T(8,128)} %get-tuple-element.210), channel_id=1, source_target_pairs={{4,0},{8,4},{12,8},{16,12},{20,16},{24,20},{28,24},{0,28},{5,1},{9... | collective-permute-start | bytes 6291464 | tf_op jit(solution)/shard_map/ppermute | solution.py:23
  1415.7 37.8 %copy-start = (f32[768,256]{1,0:T(8,128)}, f32[768,256]{1,0:T(8,128)S(1)}, u32[]{:S(2)}) copy-start(f32[768,256]{1,0:T(8,128)S(1)} %select_multiply_fusion) | copy-start | bytes 2359300
  1521.9 43.3 %slice-start = ((f32[768,256]{1,0:T(8,128)}), f32[256,256]{1,0:T(8,128)S(1)}, s32[]{:S(2)}) async-start(f32[768,256]{1,0:T(8,128)} %copy-done), calls=%async_computation.3 | async-start | bytes 524288 | tf_op jit(solution)/shard_map/slice | solution.py:81
  1521.9 43.3 %copy-start.2 = (s32[8]{0:T(128)S(1)}, s32[8]{0:T(128)}, u32[]{:S(2)}) copy-start(s32[8]{0:T(128)} %param.9) | copy-start | bytes 100
Sparse Core Ops, SparseCore 0:
  2324.9 128.4 reduce-scatter.1
where the time goes:
time: 2480 us; the launch traced here: 2460 us
  waiting for transfers between devices  848 us (34%)
  other arithmetic  814 us (33%)
  local copies, waits for them, and re-layouts  607 us (24%)
  matrix products  157 us (6%)
    all_to_all x1, waiting for transfers between devices, per_device(): lax.all_to_all(record, 'chan', split_axis=2, concat_axis=1, tiled=True)  720 us
    unnamed x9, local copies, waits for them, and re-layouts  372 us
    reduce_sum x8, other arithmetic, one_offset(): jnp.sum(own_spec[:, :, S:] * partner[:, :, :S] - own_spec[:, :, :S] * par...  334 us
    reduce_sum x8, other arithmetic, one_offset(): matched = jnp.sum(own_spec * partner, axis=0)  330 us
    reduce_scatter x1, waiting for transfers between devices, per_device(): lax.psum_scatter(lax.map(one_offset, pair_offsets), 'tm', scatter_dimensi...  129 us
    all_to_all x3, local copies, waits for them, and re-layouts, per_device(): lax.all_to_all(record, 'chan', split_axis=2, concat_axis=1, tiled=True)  116 us
    all_to_all x1, other arithmetic, per_device(): lax.all_to_all(record, 'chan', split_axis=2, concat_axis=1, tiled=True)  98.3 us
    dot_general x1, matrix products, per_device(): spectra = jnp.einsum('stc,tj->scj', whitened, forward, precision=PRECISE)  68.4 us
  transfers between devices with their start and end apart: 4, of which 2 were waited for; matrix products, arithmetic and copies ran while one was open for 4% of the time, Pallas kernels for 0%

commit v1 on v0

v1 whole, which is shorter than its diff:
```python
import functools
import math

import jax
import jax.numpy as jnp
import numpy as np
from jax import lax
from jax.experimental import pallas as pl
from jax.experimental.pallas import tpu as pltpu
from jax.sharding import PartitionSpec as P

R = 128
WIDE = 2 * R
AHEAD = 3
SLOTS = 4
ROWS = 64
LANES = 128
F32, BF16 = jnp.float32, jnp.bfloat16


def tables(seg_len, norm_scale):
    period = 2 * seg_len
    odd = 2 * np.arange(seg_len) + 1
    turn = 2.0 * math.pi / (2 * period)
    forward = np.outer(np.arange(seg_len), odd) % (2 * period) * turn
    inverse = np.outer(np.arange(seg_len) - seg_len // 2, odd) % (2 * period) * turn
    forward = np.concatenate([np.cos(forward), np.sin(forward)], axis=1)
    inverse = np.concatenate([np.cos(inverse), np.sin(inverse)], axis=1)
    return (
        forward.astype(np.float32),
        (inverse * (2.0 / period * norm_scale)).astype(np.float32),
    )


def halves(value):
    high = value.astype(BF16)
    return high, (value - high.astype(F32)).astype(BF16)


def product(left, right, dims):
    dot = lambda a, b: lax.dot_general(a, b, (dims, ((), ())), preferred_element_type=F32)
    return dot(left[0], right[0]) + (dot(left[0], right[1]) + dot(left[1], right[0]))


def kernel(
    n_chan, n_time, record, taps, offsets, forward, inv_high, inv_low, out, landed,
    spec, acc, part, inbox, xbuf, mat_high, mat_low,
    send_sem, recv_sem, load_sem, part_sem, inbox_sem,
):
    me, mine = lax.axis_index("chan"), lax.axis_index("tm")
    segs, rows, channels = record.shape
    seg_len = rows * n_chan
    block = channels // n_chan
    pieces = block // WIDE + 1
    per_time = part.shape[1] // n_time

    barrier = pltpu.get_barrier_semaphore()

    def greet_chan(r, _):
        pl.semaphore_signal(
            barrier, inc=1, device_id={"chan": lax.rem(me + r, n_chan)},
            device_id_type=pl.DeviceIdType.MESH,
        )
        return 0

    def greet_time(r, _):
        pl.semaphore_signal(
            barrier, inc=1, device_id={"tm": lax.rem(mine + r, n_time)},
            device_id_type=pl.DeviceIdType.MESH,
        )
        return 0

    lax.fori_loop(1, n_chan, greet_chan, 0)
    lax.fori_loop(1, n_time, greet_time, 0)
    pl.semaphore_wait(barrier, n_chan + n_time - 2)

    def place(piece, half, width):
        columns = pl.ds(half * R, width)
        return landed.at[piece, :, pl.ds(pl.multiple_of(me * rows, 8), rows), columns]

    def source(owner, piece, half, width):
        first = lax.rem(owner * block + piece * WIDE + half * R + (channels - R), channels)
        return record.at[:, :, pl.ds(pl.multiple_of(first, R), width)]

    def send(piece, cuts):
        for half, width in cuts:
            pltpu.make_async_copy(
                source(me, piece, half, width), place(piece, half, width), recv_sem.at[piece]
            ).start()

        def to(r, _):
            owner = lax.rem(me + r, n_chan)
            for half, width in cuts:
                pltpu.make_async_remote_copy(
                    src_ref=source(owner, piece, half, width),
                    dst_ref=place(piece, half, width),
                    send_sem=send_sem.at[piece],
                    recv_sem=recv_sem.at[piece],
                    device_id={"chan": owner},
                    device_id_type=pl.DeviceIdType.MESH,
                ).start()
            return 0

        lax.fori_loop(1, n_chan, to, 0)

    def send_any(piece):
        edge = (piece == 0) | (piece == pieces - 1)

        @pl.when(edge)
        def _():
            send(piece, ((0, R), (1, R)))

        @pl.when(jnp.logical_not(edge))
        def _():
            send(piece, ((0, WIDE),))

    for piece in range(min(AHEAD, pieces)):
        send(piece, ((0, R), (1, R)) if piece in (0, pieces - 1) else ((0, WIDE),))

    row_ids = lax.broadcasted_iota(jnp.int32, (seg_len, seg_len), 0)
    spread = lax.broadcasted_iota(jnp.int32, (seg_len, seg_len), 1) - row_ids
    acc[0, :, pl.ds(0, seg_len)] = jnp.zeros((seg_len, seg_len), F32)

    def add_tap(tap, _):
        acc[0, :, pl.ds(0, seg_len)] += jnp.where(spread == tap, taps[tap], 0.0)
        return 0

    lax.fori_loop(0, taps.shape[0], add_tap, 0)
    matrix = jnp.dot(
        acc[0, :, pl.ds(0, seg_len)], forward[...],
        precision=lax.Precision.HIGHEST, preferred_element_type=F32,
    )
    high, low = halves(matrix)
    mat_high[...] = high
    mat_low[...] = low

    def load(piece, seg):
        slot = lax.rem(seg, SLOTS)
        return pltpu.make_async_copy(landed.at[piece, seg], xbuf.at[slot], load_sem.at[slot])

    def transform(piece):
        for seg in range(SLOTS - 1):
            load(piece, seg).start()

        def one(seg, _):
            @pl.when(seg + (SLOTS - 1) < segs)
            def _():
                load(piece, seg + (SLOTS - 1)).start()

            load(piece, seg).wait()
            spec[seg, :, pl.ds(0, WIDE), :] = spec[seg, :, pl.ds(WIDE, WIDE), :]
            sample = halves(xbuf[lax.rem(seg, SLOTS)].T)
            for side in range(2):
                columns = pl.ds(side * seg_len, seg_len)
                found = product(
                    sample, (mat_high[:, columns], mat_low[:, columns]), (((1,), (0,)))
                )
                for lane in range(seg_len // LANES):
                    spec[seg, side * (seg_len // LANES) + lane, pl.ds(WIDE, WIDE), :] = found[
                        :, lane * LANES : (lane + 1) * LANES
                    ]
            return 0

        lax.fori_loop(0, segs, one, 0)

    lanes = seg_len // LANES

    def correlate(slot):
        def one_offset(k, _):
            offset = offsets[k]

            def rows_at(g, _):
                base = pl.multiple_of(g * ROWS, ROWS)
                for lane in range(lanes):
                    even = jnp.zeros((ROWS, LANES), F32)
                    odd = jnp.zeros((ROWS, LANES), F32)
                    for seg in range(segs):
                        own = pl.ds(base + R, ROWS)
                        other = pl.ds(base + R + offset, ROWS)
                        c, s = spec[seg, lane, own, :], spec[seg, lane + lanes, own, :]
                        c2, s2 = spec[seg, lane, other, :], spec[seg, lane + lanes, other, :]
                        even += c * c2 + s * s2
                        odd += c * s2 - s * c2
                    acc[k, pl.ds(base, ROWS), pl.ds(lane * LANES, LANES)] = even
                    acc[k, pl.ds(base, ROWS), pl.ds(seg_len + lane * LANES, LANES)] = odd
                return 0

            lax.fori_loop(0, WIDE // ROWS, rows_at, 0)
            part[slot, k] = product(
                (inv_high[...], inv_low[...]), halves(acc[k]), (((1,), (1,)))
            )
            return 0

        lax.fori_loop(0, part.shape[1], one_offset, 0)

    def share(i, slot):
        def to(r, _):
            peer = lax.rem(mine + r, n_time)
            pltpu.make_async_remote_copy(
                src_ref=part.at[slot, pl.ds(peer * per_time, per_time)],
                dst_ref=inbox.at[i, r - 1],
                send_sem=part_sem.at[slot],
                recv_sem=inbox_sem.at[i],
                device_id={"tm": peer},
                device_id_type=pl.DeviceIdType.MESH,
            ).start()
            return 0

        lax.fori_loop(1, n_time, to, 0)

    def wait_for(ref, sem):
        pltpu.make_async_copy(ref, ref, sem).wait()

    def finish(i):
        wait_for(inbox.at[i], inbox_sem.at[i])
        slot = lax.rem(i, 2)
        columns = pl.ds(pl.multiple_of(i * WIDE, WIDE), WIDE)
        for k in range(per_time):
            total = part[slot, mine * per_time + k]
            for r in range(n_time - 1):
                total += inbox[i, r, k]
            out[k, :, columns] = total

    def step(piece, _):
        wait_for(landed.at[piece], recv_sem.at[piece])

        @pl.when(piece + AHEAD < pieces)
        def _():
            send_any(piece + AHEAD)

        transform(piece)

        @pl.when(piece >= 1)
        def _():
            i = piece - 1
            slot = lax.rem(i, 2)

            @pl.when(i >= 2)
            def _():
                wait_for(inbox.at[i], part_sem.at[slot])

            correlate(slot)
            share(i, slot)

            @pl.when(i >= 1)
            def _():
                finish(i - 1)

        return 0

    lax.fori_loop(0, pieces, step, 0)
    finish(pieces - 2)
    for slot in range(min(2, pieces - 1)):
        wait_for(inbox.at[0], part_sem.at[slot])

    def drain(piece, _):
        wait_for(landed.at[piece, :, pl.ds(0, seg_len - rows)], send_sem.at[piece])
        return 0

    lax.fori_loop(0, pieces, drain, 0)


def per_device(record, fir_taps, pair_offsets):
    n_chan, n_time = lax.axis_size("chan"), lax.axis_size("tm")
    segs, rows, channels = record.shape
    seg_len, block, pairs = rows * n_chan, channels // n_chan, pair_offsets.shape[0]
    pieces = block // WIDE + 1
    forward, inverse = tables(seg_len, 1.0 / math.sqrt(segs * n_time * seg_len))
    inv_high = inverse.astype(jnp.bfloat16)
    inv_low = (inverse - inv_high.astype(np.float32)).astype(jnp.bfloat16)
    lanes = 2 * seg_len // LANES
    vmem, smem = pl.BlockSpec(memory_space=pltpu.VMEM), pl.BlockSpec(memory_space=pltpu.SMEM)
    anywhere = pl.BlockSpec(memory_space=pl.ANY)
    result, _ = pl.pallas_call(
        functools.partial(kernel, n_chan, n_time),
        out_shape=(
            jax.ShapeDtypeStruct((pairs // n_time, seg_len, block), F32),
            jax.ShapeDtypeStruct((pieces, segs, seg_len, WIDE), F32),
        ),
        in_specs=[anywhere, smem, smem, vmem, vmem, vmem],
        out_specs=(vmem, anywhere),
        scratch_shapes=[
            pltpu.VMEM((segs, lanes, 2 * WIDE, LANES), F32),
            pltpu.VMEM((pairs, WIDE, 2 * seg_len), F32),
            pltpu.VMEM((2, pairs, seg_len, WIDE), F32),
            pltpu.VMEM((pieces - 1, n_time - 1, pairs // n_time, seg_len, WIDE), F32),
            pltpu.VMEM((SLOTS, seg_len, WIDE), F32),
            pltpu.VMEM((seg_len, 2 * seg_len), BF16),
            pltpu.VMEM((seg_len, 2 * seg_len), BF16),
            pltpu.SemaphoreType.DMA((pieces,)),
            pltpu.SemaphoreType.DMA((pieces,)),
            pltpu.SemaphoreType.DMA((SLOTS,)),
            pltpu.SemaphoreType.DMA((2,)),
            pltpu.SemaphoreType.DMA((pieces - 1,)),
        ],
        compiler_params=pltpu.CompilerParams(
            collective_id=0, has_side_effects=True, vmem_limit_bytes=60 * 2**20
        ),
    )(record, fir_taps, pair_offsets, forward, inv_high, inv_low)
    return result


def solution(mesh):
    placed = (P("tm", "chan", None), P(), P())
    return jax.shard_map(
        per_device, mesh=mesh, in_specs=placed, out_specs=P("tm", None, "chan"), check_vma=False
    )
```

time: 2480 us -> 905 us (0.36)
  Pallas kernels: 0 us -> 900 us
  waiting for transfers between devices: 848 us -> 0 us
  other arithmetic: 814 us -> 0 us
  local copies, waits for them, and re-layouts: 607 us -> 4.7 us
  matrix products: 157 us -> 0 us
    pallas_call x0 -> x1, Pallas kernels: none -> 900 us  [per_device(): pl.pallas_call(functools.partial(kernel, n_chan, n_time), out_shape=(jax....]
    all_to_all x1 -> x0, waiting for transfers between devices: 720 us -> none  [per_device(): lax.all_to_all(record, 'chan', split_axis=2, concat_axis=1, tiled=True)]
    reduce_sum x16 -> x0, other arithmetic: 664 us -> none  [the longest x8 334 us: one_offset(): jnp.sum(own_spec[:, :, S:] * partner[:, :, :S] - own_spec[:, :, :S] * par...]
    unnamed x9 -> x1, local copies, waits for them, and re-layouts: 372 us -> 4.7 us
    dot_general x18 -> x0, matrix products: 157 us -> none  [the longest x1 68.4 us: per_device(): spectra = jnp.einsum('stc,tj->scj', whitened, forward, precision=PRECISE)]
    reduce_scatter x1 -> x0, waiting for transfers between devices: 129 us -> none  [per_device(): lax.psum_scatter(lax.map(one_offset, pair_offsets), 'tm', scatter_dimensi...]
    all_to_all x3 -> x0, local copies, waits for them, and re-layouts: 116 us -> none  [per_device(): lax.all_to_all(record, 'chan', split_axis=2, concat_axis=1, tiled=True)]
    all_to_all x1 -> x0, other arithmetic: 98.3 us -> none  [per_device(): lax.all_to_all(record, 'chan', split_axis=2, concat_axis=1, tiled=True)]
  transfers between devices with their start and end apart: 4 -> 0, of which waited for: 2 -> 0; matrix products, arithmetic and copies ran while one was open for 4% -> 0% of each run, Pallas kernels for 0% -> 0%
where the time goes in v1:
time: 905 us; the launch traced here: 904 us
  Pallas kernels  900 us (99%)
    pallas_call x1, Pallas kernels, per_device(): pl.pallas_call(functools.partial(kernel, n_chan, n_time), out_shape=(jax....  900 us

profile of v1, /device:TPU:15, one launch (start us, length us, event | category | flops | bytes accessed | tf_op | source)
XLA Modules:
  0.0 904.3 jit_solution(6913543599873935858)
XLA Ops:
  0.0 899.6 %shard_map.64 = (f32[2,256,2048]{2,1,0:T(8,128)}, f32[9,16,256,256]{3,2,1,0:T(8,128)}) custom-call(f32[16,32,16384]{2,1,0:T(8,128)} %record.1, f32[64]{0:T(128)} %taps.1, s32[8]{0:T(128)} %offsets.1, f32[256,512]{1,0:T(8,128)} %constant.6.clone.forward, bf16[256,512]{1,0:T(8,128)(2,1)} %constant.7.clone.inv_high, bf16[256,512]{1,0:T(8,128)(2,1)} %constant.8.clone.inv_low), custom_call_target="tpu_custom_call" | custom-call | tf_op jit(solution)/shard_map/pallas_call | solution.py:274
  899.6 4.7 copy.8

commit v2 on v1

--- a/solution.py
+++ b/solution.py
@@ -104,18 +104,28 @@
         lax.fori_loop(1, n_chan, to, 0)
 
     def send_any(piece):
-        edge = (piece == 0) | (piece == pieces - 1)
+        edge = piece == pieces - 1
 
         @pl.when(edge)
         def _():
-            send(piece, ((0, R), (1, R)))
+            send(piece, ((0, R),))
 
         @pl.when(jnp.logical_not(edge))
         def _():
             send(piece, ((0, WIDE),))
 
     for piece in range(min(AHEAD, pieces)):
-        send(piece, ((0, R), (1, R)) if piece in (0, pieces - 1) else ((0, WIDE),))
+        first, last = piece == 0, piece == pieces - 1
+        send(piece, ((0, R), (1, R)) if first else ((0, R),) if last else ((0, WIDE),))
+
+    edge_copy = pltpu.make_async_remote_copy(
+        src_ref=landed.at[0, :, :, pl.ds(R, R)],
+        dst_ref=landed.at[pieces - 1, :, :, pl.ds(R, R)],
+        send_sem=send_sem.at[pieces],
+        recv_sem=recv_sem.at[pieces - 1],
+        device_id={"chan": lax.rem(me + n_chan - 1, n_chan)},
+        device_id_type=pl.DeviceIdType.MESH,
+    )
 
     row_ids = lax.broadcasted_iota(jnp.int32, (seg_len, seg_len), 0)
     spread = lax.broadcasted_iota(jnp.int32, (seg_len, seg_len), 1) - row_ids
@@ -224,6 +234,10 @@
     def step(piece, _):
         wait_for(landed.at[piece], recv_sem.at[piece])
 
+        @pl.when(piece == 0)
+        def _():
+            edge_copy.start()
+
         @pl.when(piece + AHEAD < pieces)
         def _():
             send_any(piece + AHEAD)
@@ -257,7 +271,9 @@
         wait_for(landed.at[piece, :, pl.ds(0, seg_len - rows)], send_sem.at[piece])
         return 0
 
-    lax.fori_loop(0, pieces, drain, 0)
+    lax.fori_loop(0, pieces - 1, drain, 0)
+    wait_for(landed.at[pieces - 1, :, pl.ds(0, seg_len - rows), pl.ds(0, R)], send_sem.at[pieces - 1])
+    edge_copy.wait_send()
 
 
 def per_device(record, fir_taps, pair_offsets):
@@ -287,7 +303,7 @@
             pltpu.VMEM((SLOTS, seg_len, WIDE), F32),
             pltpu.VMEM((seg_len, 2 * seg_len), BF16),
             pltpu.VMEM((seg_len, 2 * seg_len), BF16),
-            pltpu.SemaphoreType.DMA((pieces,)),
+            pltpu.SemaphoreType.DMA((pieces + 1,)),
             pltpu.SemaphoreType.DMA((pieces,)),
             pltpu.SemaphoreType.DMA((SLOTS,)),
             pltpu.SemaphoreType.DMA((2,)),

time: 905 us -> 898 us (level)
  Pallas kernels: 900 us -> 886 us
    pallas_call x1, Pallas kernels: 900 us -> 886 us  [per_device(): pl.pallas_call(functools.partial(kernel, n_chan, n_time), out_shape=(jax....]
where the time goes in v2:
time: 898 us; the launch traced here: 891 us
  Pallas kernels  886 us (99%)
    pallas_call x1, Pallas kernels, per_device(): pl.pallas_call(functools.partial(kernel, n_chan, n_time), out_shape=(jax....  886 us

profile of v2, /device:TPU:15, one launch (start us, length us, event | category | flops | bytes accessed | tf_op | source)
XLA Modules:
  0.0 890.7 jit_solution(15627020766258128170)
XLA Ops:
  0.0 886.0 %shard_map.64 = (f32[2,256,2048]{2,1,0:T(8,128)}, f32[9,16,256,256]{3,2,1,0:T(8,128)}) custom-call(f32[16,32,16384]{2,1,0:T(8,128)} %record.1, f32[64]{0:T(128)} %taps.1, s32[8]{0:T(128)} %offsets.1, f32[256,512]{1,0:T(8,128)} %constant.6.clone.forward, bf16[256,512]{1,0:T(8,128)(2,1)} %constant.7.clone.inv_high, bf16[256,512]{1,0:T(8,128)(2,1)} %constant.8.clone.inv_low), custom_call_target="tpu_custom_call" | custom-call | tf_op jit(solution)/shard_map/pallas_call | solution.py:290
  886.0 4.7 copy.8
